TPU v7x, 32 devices: a whole 2x2x4 slice. The times are simulated.
32 devices in a mesh: particle: 8 (over z, x), token: 4 (over y, core).
Axes of the slice: x: 2, y: 2, z: 4, core: 2. Of those that a mesh axis runs over, the one named last changes fastest.
Arguments:
- states: bfloat16 [16, 256, 768], P('particle', 'token'), may hold values from -6 to 6
- ancestors: int32 [16], P('particle'), may hold values from 0 to 15, as said below
- pair_bias: bfloat16 [16, 256, 256], P(None, 'token'), may hold values from -3 to 300, as said below
- key_mask: int32 [256], replicated, may hold values from 0 to 1, as said below
- gain_attn: float32 [768], replicated, may hold values from 0.1 to 1.9
- w_qkv: bfloat16 [768, 2304], replicated, may hold values from -0.21875 to 0.21875
- w_o: bfloat16 [768, 768], replicated, may hold values from -0.21875 to 0.21875
- gain_ff: float32 [768], replicated, may hold values from 0.1 to 1.9
- w_in: bfloat16 [2, 768, 1536], P(None, 'particle'), may hold values from -0.21875 to 0.21875
- w_out: bfloat16 [768, 1536], P('particle'), may hold values from -0.15625 to 0.15625
Outputs:
- new_states: bfloat16 [16, 256, 768], P('particle', 'token')
Inputs may be any that keep to these rules, and one draw needn't show every extreme that they name: `ancestors`: any particle may be the ancestor of any number of particles. `pair_bias`: real values; rows of some heads may hold a few large entries. `key_mask`: 1 on a prefix of 128 or more tokens and 0 after it; the last token is always 0.
All inputs are finite; a program needn't handle non-finite values.
Results may differ from a plain program's by a relative error of at most 0.0085.
Values may be sent and summed in bfloat16 or wider, within the bound.
A program may use at most 64 MiB of HBM per device.

v0:
```python
import math

import jax
import jax.numpy as jnp
from jax import lax
from jax.experimental import pallas as pl
from jax.experimental.pallas import tpu as pltpu
from jax.sharding import PartitionSpec as P

MESH = pl.DeviceIdType.MESH


def rms_norm(stream, gain_vec):
    return stream * lax.rsqrt(jnp.mean(stream * stream, axis=-1, keepdims=True) + 1e-05) * gain_vec


def attend_portion(running_sum, queries, key_part, value_part, pair_bias, key_mask):
    running, totals, summed = running_sum
    part_count, row_count, model_width = queries.shape
    head_count = pair_bias.shape[0]
    head_size = model_width // head_count
    number = key_part.shape[1]
    query_heads = queries.reshape(part_count, row_count, head_count, head_size)
    key_heads = key_part.reshape(part_count, number, head_count, head_size)
    value_heads = value_part.reshape(part_count, number, head_count, head_size)
    scores = jnp.einsum(
        "prhe,pnhe->phrn", query_heads, key_heads, preferred_element_type=jnp.float32
    )
    bias_part = pair_bias.astype(jnp.float32)
    scores = scores + bias_part[None]
    usable = (key_mask > 0)[None, None, None, :]
    new_max = jnp.maximum(running, jnp.max(jnp.where(usable, scores, -1e30), axis=3))
    weights = jnp.where(usable, jnp.exp(scores - new_max[..., None]), 0.0)
    totals = jnp.sum(weights, axis=3)
    summed = jnp.einsum(
        "phrn,pnhe->phre",
        weights.astype(jnp.bfloat16),
        value_heads,
        preferred_element_type=jnp.float32,
    )
    return (new_max, totals, summed)


def run_block(states, pair_bias, key_mask, gain_attn, w_qkv, w_o, gain_ff, w_in, w_out):
    part_count, row_count, model_width = states.shape
    head_count = pair_bias.shape[0]
    head_size = model_width // head_count
    score_scale = 1.0 / math.sqrt(head_size)
    stream = states.astype(jnp.float32)
    normed = rms_norm(stream, gain_attn).astype(jnp.bfloat16)
    start_carry = (
        jnp.full((part_count, head_count, row_count), -1e30, jnp.float32),
        jnp.zeros((part_count, head_count, row_count), jnp.float32),
        jnp.zeros((part_count, head_count, row_count, head_size), jnp.float32),
    )
    queries = (
        jnp.einsum(
            "prd,de->pre", normed, w_qkv[:, :model_width], preferred_element_type=jnp.float32
        )
        * score_scale
    ).astype(jnp.bfloat16)
    normed_all = lax.all_gather(normed, "token", axis=1, tiled=True)
    projected = jnp.einsum(
        "prd,de->pre", normed_all, w_qkv[:, model_width:], preferred_element_type=jnp.float32
    ).astype(jnp.bfloat16)
    portion = (projected[..., :model_width], projected[..., model_width:])
    running, totals, summed = attend_portion(
        start_carry, queries, portion[0], portion[1], pair_bias, key_mask
    )
    attended = (
        (summed / totals[..., None])
        .transpose(0, 2, 1, 3)
        .reshape(part_count, row_count, model_width)
        .astype(jnp.bfloat16)
    )
    stream = stream + jnp.einsum("prd,de->pre", attended, w_o, preferred_element_type=jnp.float32)
    normed_ff = rms_norm(stream, gain_ff).astype(jnp.bfloat16)
    normed_ff = lax.all_gather(normed_ff, "token", axis=1, tiled=True)
    gate_sum = jnp.einsum("prd,df->prf", normed_ff, w_in[0], preferred_element_type=jnp.float32)
    up_sum = jnp.einsum("prd,df->prf", normed_ff, w_in[1], preferred_element_type=jnp.float32)
    hidden = (jax.nn.silu(gate_sum) * up_sum).astype(jnp.bfloat16)
    update = jnp.einsum(
        "prf,nf->prn", hidden, w_out, preferred_element_type=jnp.float32
    ).astype(jnp.bfloat16)
    update = lax.psum_scatter(update, "token", scatter_dimension=1, tiled=True)
    return (stream + update.astype(jnp.float32)).astype(jnp.bfloat16)


def select_rows(ancestors, portion):
    number = portion.shape[0]
    indices = lax.iota(jnp.int32, number)
    onehot = (ancestors[:, None] == indices[None, :]).astype(jnp.bfloat16)
    return jnp.einsum("jp,prd->jrd", onehot, portion, preferred_element_type=jnp.float32)


def body(states, ancestors, pair_bias, key_mask, gain_attn, w_qkv, w_o, gain_ff, w_in, w_out):
    chosen = select_rows(ancestors, lax.all_gather(states, "particle", axis=0, tiled=True)).astype(
        jnp.bfloat16
    )
    units = w_out.shape[1] // lax.axis_size("token")
    first = lax.axis_index("token") * units
    w_in = lax.all_gather(
        lax.dynamic_slice_in_dim(w_in, first, units, 2), "particle", axis=1, tiled=True
    )
    w_out = lax.all_gather(
        lax.dynamic_slice_in_dim(w_out, first, units, 1), "particle", axis=0, tiled=True
    )
    return run_block(chosen, pair_bias, key_mask, gain_attn, w_qkv, w_o, gain_ff, w_in, w_out)


def block_kernel(
    states_ref, ancestors_ref, bias_hbm, mask_ref, gain_attn_ref, w_qkv_hbm, w_o_hbm, gain_ff_ref,
    w_in_hbm, w_out_hbm, out_ref,
    states_all, w_in_all, w_out_all, w_qkv, w_o, bias, normed_all, kv_all, ff_all,
    core_out, core_in, row_out, row_in, wish_out, wish_in, pick_out, pick_in,
    local_sem, recv_sem, right_sem, left_sem, across_sem, gather_recv, gather_row, gather_core,
    core_send, core_recv, row_send, row_recv, wish_send, wish_recv, pick_send, pick_recv,
):
    per, rows, width = states_ref.shape
    groups = lax.axis_size("particle")
    lines = groups // 2
    cells = lax.axis_size("token")
    spans = cells // 2
    units = w_in_all.shape[-1]
    head_count = bias.shape[0] // rows
    head_size = width // head_count
    me = lax.axis_index("particle")
    spot = lax.axis_index("token")
    line, side = me // 2, me % 2
    span, core = spot // 2, spot % 2
    across = (line * 2 + 1 - side, spot)
    above, below = (me + 2, spot), (me - 2, spot)
    other_core = (me, span * 2 + 1 - core)

    def span_peer(step):
        return lax.rem(span + step, spans)

    barrier = pltpu.get_barrier_semaphore()

    def greet(device):
        pl.semaphore_signal(barrier, inc=1, device_id=device, device_id_type=MESH)

    greet(across)
    greet(other_core)
    for step in range(1, spans):
        greet((me, span_peer(step) * 2 + core))

    @pl.when(line > 0)
    def _():
        greet(below)

    @pl.when(line < lines - 1)
    def _():
        greet(above)

    first = pl.multiple_of(spot * units, 128)
    locals_ = [
        pltpu.make_async_copy(states_ref, states_all.at[pl.ds(me * per, per)], local_sem.at[0]),
        pltpu.make_async_copy(
            w_in_hbm.at[:, :, pl.ds(first, units)], w_in_all.at[me], local_sem.at[1]
        ),
        pltpu.make_async_copy(
            w_out_hbm.at[:, pl.ds(first, units)], w_out_all.at[me], local_sem.at[2]
        ),
        pltpu.make_async_copy(w_qkv_hbm, w_qkv, local_sem.at[3]),
        pltpu.make_async_copy(bias_hbm, bias, local_sem.at[4]),
        pltpu.make_async_copy(w_o_hbm, w_o, local_sem.at[5]),
    ]
    for copy in locals_:
        copy.start()
    locals_[0].wait()
    pl.semaphore_wait(
        barrier,
        2 + spans - 1 + jnp.where(line > 0, 1, 0) + jnp.where(line < lines - 1, 1, 0),
    )

    views = (
        lambda k: states_all.at[pl.ds(k * per, per)],
        lambda k: w_in_all.at[k],
        lambda k: w_out_all.at[k],
    )

    def remote(kind, source, sems, device):
        k = source * 2 + side
        return pltpu.make_async_remote_copy(
            src_ref=views[kind](k),
            dst_ref=views[kind](k),
            send_sem=sems.at[kind, source],
            recv_sem=recv_sem.at[kind, k],
            device_id=device,
            device_id_type=MESH,
        )

    def arrived(kind, k):
        pltpu.make_async_remote_copy(
            src_ref=views[kind](k),
            dst_ref=views[kind](k),
            send_sem=across_sem.at[kind, 0],
            recv_sem=recv_sem.at[kind, k],
            device_id=across,
            device_id_type=MESH,
        ).wait_recv()

    def relay(kind, step, along=True, cross=True):
        low, high = line - step, line + step

        @pl.when(low >= 0)
        def _():
            if step > 0:
                arrived(kind, low * 2 + side)

            @pl.when(jnp.logical_and(along, line < lines - 1))
            def _():
                remote(kind, low, right_sem, above).start()

        @pl.when(high < lines)
        def _():
            if step > 0:
                arrived(kind, high * 2 + side)

            @pl.when(jnp.logical_and(along, line > 0))
            def _():
                remote(kind, high, left_sem, below).start()

        if kind == 0 or not cross:
            return

        @pl.when(low >= 0)
        def _():
            remote(kind, low, across_sem, across).start()

        if step > 0:

            @pl.when(high < lines)
            def _():
                remote(kind, high, across_sem, across).start()

    def finish(kind):
        for source in range(lines):
            arrived(kind, source * 2 + 1 - side)

    def drain(kind):
        for source in range(lines):
            if kind > 0:
                remote(kind, source, across_sem, across).wait_send()

            @pl.when(jnp.logical_and(line < lines - 1, source <= line))
            def _():
                remote(kind, source, right_sem, above).wait_send()

            @pl.when(jnp.logical_and(line > 0, source >= line))
            def _():
                remote(kind, source, left_sem, below).wait_send()

    def slot_copy(which, buf, j, slot, send, device):
        return pltpu.make_async_remote_copy(
            src_ref=buf.at[j, slot],
            dst_ref=buf.at[j, slot],
            send_sem=send,
            recv_sem=gather_recv.at[which, j, slot],
            device_id=device,
            device_id_type=MESH,
        )

    sent = []

    def token_sends(which, buf, j):
        for step in range(1, spans):
            device = (me, span_peer(step) * 2 + core)
            sent.append(slot_copy(which, buf, j, spot, gather_row.at[which, j, step], device))
            sent[-1].start()
        sent.append(slot_copy(which, buf, j, spot, gather_core.at[which, j, 0], other_core))
        sent[-1].start()

    def token_forward(which, buf, j):
        for step in range(1, spans):
            slot = span_peer(step) * 2 + core
            copy = slot_copy(which, buf, j, slot, gather_core.at[which, j, step], other_core)
            copy.wait_recv()
            copy.start()
            sent.append(copy)

    def token_finish(which, buf, j):
        for step in range(spans):
            slot = span_peer(step) * 2 + 1 - core
            slot_copy(
                which, buf, j, slot, gather_core.at[which, j, 0], other_core
            ).wait_recv()

    def norm(stream, gain):
        mean = jnp.mean(stream * stream, axis=-1, keepdims=True)
        return (stream * lax.rsqrt(mean + 1e-05) * gain).astype(jnp.bfloat16)

    def dot(a, b):
        return jnp.dot(a, b, preferred_element_type=jnp.float32)

    def dot_t(a, b):
        return lax.dot_general(
            a, b, (((1,), (1,)), ((), ())), preferred_element_type=jnp.float32
        )

    tokens = cells * rows
    last = lines - 1
    for j in range(per):
        wish_out[j] = jnp.full(wish_out.shape[1:], ancestors_ref[j], jnp.int32)

    def to_across(source, target, send, recv):
        return pltpu.make_async_remote_copy(
            src_ref=source,
            dst_ref=target,
            send_sem=send,
            recv_sem=recv,
            device_id=across,
            device_id_type=MESH,
        )

    wish = to_across(wish_out, wish_in, wish_send, wish_recv)
    wish.start()
    relay(0, 0)
    locals_[1].wait()
    relay(1, 0, along=False)
    locals_[2].wait()
    relay(2, 0, along=False)
    wish.wait_recv()

    def pick_from(found, wished, source):
        for i in range(per):
            k = (source * 2 + side) * per + i
            found = jnp.where(wished[:1, :1] == k, states_all[k].astype(jnp.float32), found)
        return found

    nothing = jnp.zeros((rows, width), jnp.float32)
    asked = [pick_from(nothing, wish_in[j], line) for j in range(per)]
    for step in range(1, lines):
        relay(0, step)
        if step == last - 1:
            relay(1, 0, cross=False)
        for source in (jnp.maximum(line - step, 0), jnp.minimum(line + step, last)):
            if step < last:
                asked = [pick_from(asked[j], wish_in[j], source) for j in range(per)]
    picks = []
    for j in range(per):
        if last > 0:
            for source in (0, last):
                asked[j] = pick_from(asked[j], wish_in[j], source)
        pick_out[j] = asked[j].astype(jnp.bfloat16)
        picks.append(to_across(pick_out.at[j], pick_in.at[j], pick_send.at[j], pick_recv.at[j]))
        picks[j].start()
    own = []
    for j in range(per):
        found = nothing
        for source in range(lines):
            found = pick_from(found, wish_out[j], source)
        own.append(found)

    gain = gain_attn_ref[...].reshape(1, width)
    streams, normed = [], []
    for j in range(per):
        picks[j].wait_recv()
        streams.append(own[j] + pick_in[j].astype(jnp.float32))
        normed.append(norm(streams[j], gain))
        normed_all[j, spot] = normed[j]
        token_sends(0, normed_all, j)
    locals_[3].wait()
    scale = 1.0 / math.sqrt(head_size)
    queries = (dot(jnp.concatenate(normed, axis=0), w_qkv[:, :width]) * scale).astype(jnp.bfloat16)
    token_forward(0, normed_all, 0)
    if lines > 1:
        relay(1, 1)

    usable = mask_ref[...].reshape(1, -1) > 0
    half = 8
    strip = half * head_size
    lane = lax.broadcasted_iota(jnp.int32, (half, 1, strip), 2)
    head = lax.broadcasted_iota(jnp.int32, (half, 1, strip), 0)
    mine = jnp.logical_and(lane >= head * head_size, lane < (head + 1) * head_size)
    mine_f = mine.astype(jnp.float32)
    mine_bf = mine_f.astype(jnp.bfloat16)

    def make_keys(j):
        kv_all[j] = dot(normed_all[j].reshape(tokens, width), w_qkv[:, width:]).astype(
            jnp.bfloat16
        )

    def attend(j):
        strips = []
        for part in range(head_count // half):
            low, high = part * strip, (part + 1) * strip
            q = queries[j * rows : (j + 1) * rows, low:high]
            spread = (q[None] * mine_bf).reshape(half * rows, strip)
            scores = dot_t(spread, kv_all[j, :, low:high]) + bias[
                part * half * rows : (part + 1) * half * rows, :
            ].astype(jnp.float32)
            scores = jnp.where(usable, scores, -1e30)
            weights = jnp.exp(scores - jnp.max(scores, axis=1, keepdims=True))
            total = jnp.sum(weights, axis=1, keepdims=True)
            mix = dot(weights.astype(jnp.bfloat16), kv_all[j, :, width + low : width + high])
            mix = mix * (1.0 / total)
            strips.append(jnp.sum(mix.reshape(half, rows, strip) * mine_f, axis=0))
        return jnp.concatenate(strips, axis=1).astype(jnp.bfloat16)

    def close(j, attended):
        streams[j] = streams[j] + dot(attended, w_o[...])
        ff_all[j, spot] = norm(streams[j], gain_ff_ref[...].reshape(1, width))
        token_sends(1, ff_all, j)

    token_finish(0, normed_all, 0)
    make_keys(0)
    for j in range(1, per):
        token_forward(0, normed_all, j)
    for step in range(2, last):
        relay(1, step)
    relay(2, 0, cross=False)
    locals_[4].wait()
    attended = attend(0)
    locals_[5].wait()
    close(0, attended)
    if lines > 2:
        relay(1, last)
    for j in range(1, per):
        token_finish(0, normed_all, j)
        make_keys(j)
        if j == 1 and lines > 1:
            relay(2, 1)
        attended = attend(j)
        token_forward(1, ff_all, j - 1)
        close(j, attended)
    for step in range(2, lines):
        relay(2, step)
    finish(1)

    is_low = core == 0
    kept, cored, rowed = [], [], []

    def to_core(j):
        return pltpu.make_async_remote_copy(
            src_ref=core_out.at[j],
            dst_ref=core_in.at[j],
            send_sem=core_send.at[j],
            recv_sem=core_recv.at[j],
            device_id=other_core,
            device_id_type=MESH,
        )

    def to_row(j, step):
        return pltpu.make_async_remote_copy(
            src_ref=row_out.at[j, span_peer(step)],
            dst_ref=row_in.at[j, step],
            send_sem=row_send.at[j, step],
            recv_sem=row_recv.at[j, step],
            device_id=(me, span_peer(step) * 2 + core),
            device_id_type=MESH,
        )

    def send_rows(j):
        cored[j].wait_recv()
        row_out[j] = (kept[j] + core_in[j].astype(jnp.float32)).astype(jnp.bfloat16)
        for step in range(1, spans):
            rowed.append(to_row(j, step))
            rowed[-1].start()

    for j in range(per):
        token_finish(1, ff_all, j)
        normed_ff = ff_all[j].reshape(tokens, width)
        gate = dot(normed_ff, w_in_all[:, 0].reshape(width, units))
        up = dot(normed_ff, w_in_all[:, 1].reshape(width, units))
        hidden = (gate / (1.0 + jnp.exp(-gate)) * up).astype(jnp.bfloat16)
        if j == 0:
            finish(2)
        if j + 1 == per - 1:
            token_forward(1, ff_all, per - 1)
        if j > 0:
            send_rows(j - 1)
        update = dot_t(hidden, w_out_all[...].reshape(width, units))
        update = update.reshape(spans, 2, rows, width)
        core_out[j] = jnp.where(is_low, update[:, 1], update[:, 0]).astype(jnp.bfloat16)
        cored.append(to_core(j))
        cored[j].start()
        kept.append(jnp.where(is_low, update[:, 0], update[:, 1]))
    send_rows(per - 1)
    for j in range(per):
        stream = streams[j] + row_out[j, span].astype(jnp.float32)
        for step in range(1, spans):
            to_row(j, step).wait_recv()
            stream = stream + row_in[j, step].astype(jnp.float32)
        out_ref[j] = stream.astype(jnp.bfloat16)
    for copy in sent + cored + rowed + [wish] + picks:
        copy.wait_send()
    for kind in range(3):
        drain(kind)


def fused_body(
    states, ancestors, pair_bias, key_mask, gain_attn, w_qkv, w_o, gain_ff, w_in, w_out
):
    per, rows, width = states.shape
    groups, cells = lax.axis_size("particle"), lax.axis_size("token")
    lines, spans = groups // 2, cells // 2
    units = w_out.shape[1] // cells
    depth = w_in.shape[1]
    heads, _, keys = pair_bias.shape
    vmem = pl.BlockSpec(memory_space=pltpu.VMEM)
    smem = pl.BlockSpec(memory_space=pltpu.SMEM)
    hbm = pl.BlockSpec(memory_space=pl.ANY)
    dma = pltpu.SemaphoreType.DMA
    bf16 = jnp.bfloat16
    block = (rows, width)
    return pl.pallas_call(
        block_kernel,
        out_shape=jax.ShapeDtypeStruct(states.shape, bf16),
        in_specs=[vmem, smem, hbm, vmem, vmem, hbm, hbm, vmem, hbm, hbm],
        out_specs=vmem,
        scratch_shapes=[
            pltpu.VMEM((groups * per, rows, width), bf16),
            pltpu.VMEM((groups, 2, depth, units), bf16),
            pltpu.VMEM((groups, depth, units), bf16),
            pltpu.VMEM(w_qkv.shape, bf16),
            pltpu.VMEM(w_o.shape, bf16),
            pltpu.VMEM((heads * rows, keys), bf16),
            pltpu.VMEM((per, cells) + block, bf16),
            pltpu.VMEM((per, cells * rows, 2 * width), bf16),
            pltpu.VMEM((per, cells) + block, bf16),
            pltpu.VMEM((per, spans) + block, bf16),
            pltpu.VMEM((per, spans) + block, bf16),
            pltpu.VMEM((per, spans) + block, bf16),
            pltpu.VMEM((per, spans) + block, bf16),
            pltpu.VMEM((per, 8, 128), jnp.int32),
            pltpu.VMEM((per, 8, 128), jnp.int32),
            pltpu.VMEM((per, rows, width), bf16),
            pltpu.VMEM((per, rows, width), bf16),
            dma((6,)),
            dma((3, groups)),
            dma((3, lines)),
            dma((3, lines)),
            dma((3, lines)),
            dma((2, per, cells)),
            dma((2, per, spans)),
            dma((2, per, spans)),
            dma((per,)),
            dma((per,)),
            dma((per, spans)),
            dma((per, spans)),
            dma,
            dma,
            dma((per,)),
            dma((per,)),
        ],
        compiler_params=pltpu.CompilerParams(
            collective_id=0, has_side_effects=True, vmem_limit_bytes=56 * 1024 * 1024
        ),
    )(
        states,
        ancestors,
        pair_bias.reshape(heads * rows, keys),
        key_mask,
        gain_attn,
        w_qkv,
        w_o,
        gain_ff,
        w_in,
        w_out,
    )


def either_body(states, ancestors, pair_bias, key_mask, gain_attn, w_qkv, w_o, gain_ff, w_in, w_out):
    tiles = w_in.shape[1] % 16 == 0 and (w_out.shape[1] // lax.axis_size("token")) % 128 == 0
    run = fused_body if tiles else body
    return run(
        states, ancestors, pair_bias, key_mask, gain_attn, w_qkv, w_o, gain_ff, w_in, w_out
    )


def solution(mesh):
    placed = (
        P("particle", "token", None),
        P("particle"),
        P(None, "token", None),
        P(),
        P(),
        P(),
        P(),
        P(),
        P(None, "particle", None),
        P("particle", None),
    )
    return jax.shard_map(
        either_body, mesh=mesh, in_specs=placed, out_specs=P("particle", "token", None), check_vma=False
    )
```

profile of v0, /device:TPU:0, one launch (start us, length us, event | category | flops | bytes accessed | tf_op | source)
XLA Modules:
  0.0 56.6 jit_solution(12244135577308474931)
XLA Ops:
  0.0 54.9 %shard_map.100 = bf16[2,64,768]{2,1,0:T(8,128)(2,1)} custom-call(bf16[2,64,768]{2,1,0:T(8,128)(2,1)} %states_ref.1, s32[2]{0:T(128)} %ancestors_ref.1, bf16[1024,256]{1,0:T(8,128)(2,1)} %bitcast.1, s32[256]{0:T(256)} %mask_ref.1, f32[768]{0:T(1024)} %gain_attn_ref.1, bf16[768,2304]{1,0:T(8,128)(2,1)} %w_qkv_hbm.1, bf16[768,768]{1,0:T(8,128)(2,1)} %w_o_hbm.1, ...), custom_call_target="tpu_custom_call" | custom-call | tf_op jit(solution)/shard_map/pallas_call | solution.py:508
  54.9 1.6 %copy.12 = bf16[2,64,768]{2,1,0:T(8,128)(2,1)} copy(bf16[2,64,768]{2,1,0:T(8,128)(2,1)} %shard_map.100) | data formatting | bytes 393216
where the time goes:
time: 57.4 us; the launch traced here: 56.6 us
  Pallas kernels  54.9 us (96%)
  local copies, waits for them, and re-layouts  1.62 us (3%)
    pallas_call x1, Pallas kernels, fused_body(): pl.pallas_call(block_kernel, out_shape=jax.ShapeDtypeStruct(states.shape,...  54.9 us
    unnamed x1, local copies, waits for them, and re-layouts  1.62 us

commit v1 on v0

--- a/solution.py
+++ b/solution.py
@@ -314,6 +314,15 @@
             device_id_type=MESH,
         )
 
+    def own_weights_along(step):
+        @pl.when(jnp.logical_and(line == step, line < last))
+        def _():
+            remote(1, line, right_sem, above).start()
+
+        @pl.when(jnp.logical_and(line == last - step, line > 0))
+        def _():
+            remote(1, line, left_sem, below).start()
+
     wish = to_across(wish_out, wish_in, wish_send, wish_recv)
     wish.start()
     relay(0, 0)
@@ -321,6 +330,7 @@
     relay(1, 0, along=False)
     locals_[2].wait()
     relay(2, 0, along=False)
+    own_weights_along(0)
     wish.wait_recv()
 
     def pick_from(found, wished, source):
@@ -333,8 +343,7 @@
     asked = [pick_from(nothing, wish_in[j], line) for j in range(per)]
     for step in range(1, lines):
         relay(0, step)
-        if step == last - 1:
-            relay(1, 0, cross=False)
+        own_weights_along(step)
         for source in (jnp.maximum(line - step, 0), jnp.minimum(line + step, last)):
             if step < last:
                 asked = [pick_from(asked[j], wish_in[j], source) for j in range(per)]
@@ -352,6 +361,8 @@
         for source in range(lines):
             found = pick_from(found, wish_out[j], source)
         own.append(found)
+    if lines > 1:
+        relay(1, 1)
 
     gain = gain_attn_ref[...].reshape(1, width)
     streams, normed = [], []
@@ -365,8 +376,9 @@
     scale = 1.0 / math.sqrt(head_size)
     queries = (dot(jnp.concatenate(normed, axis=0), w_qkv[:, :width]) * scale).astype(jnp.bfloat16)
     token_forward(0, normed_all, 0)
-    if lines > 1:
-        relay(1, 1)
+    for step in range(2, last):
+        relay(1, step)
+    relay(2, 0, cross=False)
 
     usable = mask_ref[...].reshape(1, -1) > 0
     half = 8
@@ -408,25 +420,25 @@
     make_keys(0)
     for j in range(1, per):
         token_forward(0, normed_all, j)
-    for step in range(2, last):
-        relay(1, step)
-    relay(2, 0, cross=False)
     locals_[4].wait()
     attended = attend(0)
     locals_[5].wait()
     close(0, attended)
     if lines > 2:
         relay(1, last)
+    if lines > 1:
+        relay(2, 1)
     for j in range(1, per):
         token_finish(0, normed_all, j)
         make_keys(j)
-        if j == 1 and lines > 1:
-            relay(2, 1)
+        if j == 1:
+            for step in range(2, last):
+                relay(2, step)
         attended = attend(j)
         token_forward(1, ff_all, j - 1)
         close(j, attended)
-    for step in range(2, lines):
-        relay(2, step)
+    if lines > 2:
+        relay(2, last)
     finish(1)
 
     is_low = core == 0

time: 57.4 us -> 56.4 us (0.983); the launches traced: 56.6 us -> 56.2 us
  no operation moved by 1% of the time
where the time goes in v1:
time: 56.4 us; the launch traced here: 56.2 us
  Pallas kernels  54.6 us (97%)
  local copies, waits for them, and re-layouts  1.62 us (3%)
    pallas_call x1, Pallas kernels, fused_body(): pl.pallas_call(block_kernel, out_shape=jax.ShapeDtypeStruct(states.shape,...  54.6 us
    unnamed x1, local copies, waits for them, and re-layouts  1.62 us

profile of v1, /device:TPU:0, one launch (start us, length us, event | category | flops | bytes accessed | tf_op | source)
XLA Modules:
  0.0 56.2 jit_solution(8867766259339260536)
XLA Ops:
  0.0 54.6 %shard_map.100 = bf16[2,64,768]{2,1,0:T(8,128)(2,1)} custom-call(bf16[2,64,768]{2,1,0:T(8,128)(2,1)} %states_ref.1, s32[2]{0:T(128)} %ancestors_ref.1, bf16[1024,256]{1,0:T(8,128)(2,1)} %bitcast.1, s32[256]{0:T(256)} %mask_ref.1, f32[768]{0:T(1024)} %gain_attn_ref.1, bf16[768,2304]{1,0:T(8,128)(2,1)} %w_qkv_hbm.1, bf16[768,768]{1,0:T(8,128)(2,1)} %w_o_hbm.1, ...), custom_call_target="tpu_custom_call" | custom-call | tf_op jit(solution)/shard_map/pallas_call | solution.py:520
  54.6 1.6 %copy.12 = bf16[2,64,768]{2,1,0:T(8,128)(2,1)} copy(bf16[2,64,768]{2,1,0:T(8,128)(2,1)} %shard_map.100) | data formatting | bytes 393216

commit v2 on v1

--- a/solution.py
+++ b/solution.py
@@ -280,8 +280,8 @@
             copy.start()
             sent.append(copy)
 
-    def token_finish(which, buf, j):
-        for step in range(spans):
+    def token_finish(which, buf, j, steps=range(spans)):
+        for step in steps:
             slot = span_peer(step) * 2 + 1 - core
             slot_copy(
                 which, buf, j, slot, gather_core.at[which, j, 0], other_core
@@ -373,8 +373,17 @@
         normed_all[j, spot] = normed[j]
         token_sends(0, normed_all, j)
     locals_[3].wait()
+
+    def make_span_keys(j, step):
+        start = span_peer(step) * 2
+        kv_all[j, pl.ds(pl.multiple_of(start * rows, 2 * rows), 2 * rows)] = dot(
+            normed_all[j, pl.ds(start, 2)].reshape(2 * rows, width), w_qkv[:, width:]
+        ).astype(jnp.bfloat16)
+
     scale = 1.0 / math.sqrt(head_size)
     queries = (dot(jnp.concatenate(normed, axis=0), w_qkv[:, :width]) * scale).astype(jnp.bfloat16)
+    token_finish(0, normed_all, 0, range(1))
+    make_span_keys(0, 0)
     token_forward(0, normed_all, 0)
     for step in range(2, last):
         relay(1, step)
@@ -416,8 +425,9 @@
         ff_all[j, spot] = norm(streams[j], gain_ff_ref[...].reshape(1, width))
         token_sends(1, ff_all, j)
 
-    token_finish(0, normed_all, 0)
-    make_keys(0)
+    token_finish(0, normed_all, 0, range(1, spans))
+    for step in range(1, spans):
+        make_span_keys(0, step)
     for j in range(1, per):
         token_forward(0, normed_all, j)
     locals_[4].wait()
@@ -437,8 +447,6 @@
         attended = attend(j)
         token_forward(1, ff_all, j - 1)
         close(j, attended)
-    if lines > 2:
-        relay(2, last)
     finish(1)
 
     is_low = core == 0
@@ -478,6 +486,8 @@
         up = dot(normed_ff, w_in_all[:, 1].reshape(width, units))
         hidden = (gate / (1.0 + jnp.exp(-gate)) * up).astype(jnp.bfloat16)
         if j == 0:
+            if lines > 2:
+                relay(2, last)
             finish(2)
         if j + 1 == per - 1:
             token_forward(1, ff_all, per - 1)

time: 56.4 us -> 55.8 us (0.989)
  no operation moved by 1% of the time
where the time goes in v2:
time: 55.8 us; the launch traced here: 55.7 us
  Pallas kernels  54.1 us (97%)
  local copies, waits for them, and re-layouts  1.62 us (3%)
    pallas_call x1, Pallas kernels, fused_body(): pl.pallas_call(block_kernel, out_shape=jax.ShapeDtypeStruct(states.shape,...  54.1 us
    unnamed x1, local copies, waits for them, and re-layouts  1.62 us

profile of v2, /device:TPU:0, one launch (start us, length us, event | category | flops | bytes accessed | tf_op | source)
XLA Modules:
  0.0 55.7 jit_solution(14950432512203298617)
XLA Ops:
  0.0 54.1 %shard_map.100 = bf16[2,64,768]{2,1,0:T(8,128)(2,1)} custom-call(bf16[2,64,768]{2,1,0:T(8,128)(2,1)} %states_ref.1, s32[2]{0:T(128)} %ancestors_ref.1, bf16[1024,256]{1,0:T(8,128)(2,1)} %bitcast.1, s32[256]{0:T(256)} %mask_ref.1, f32[768]{0:T(1024)} %gain_attn_ref.1, bf16[768,2304]{1,0:T(8,128)(2,1)} %w_qkv_hbm.1, bf16[768,768]{1,0:T(8,128)(2,1)} %w_o_hbm.1, ...), custom_call_target="tpu_custom_call" | custom-call | tf_op jit(solution)/shard_map/pallas_call | solution.py:530
  54.1 1.6 %copy.12 = bf16[2,64,768]{2,1,0:T(8,128)(2,1)} copy(bf16[2,64,768]{2,1,0:T(8,128)(2,1)} %shard_map.100) | data formatting | bytes 393216

commit v3 on v2

--- a/solution.py
+++ b/solution.py
@@ -450,14 +450,14 @@
     finish(1)
 
     is_low = core == 0
-    kept, cored, rowed = [], [], []
-
-    def to_core(j):
+    cored, rowed = [], []
+
+    def to_core(j, spans_of, sem):
         return pltpu.make_async_remote_copy(
-            src_ref=core_out.at[j],
-            dst_ref=core_in.at[j],
-            send_sem=core_send.at[j],
-            recv_sem=core_recv.at[j],
+            src_ref=core_out.at[j, spans_of],
+            dst_ref=core_in.at[j, spans_of],
+            send_sem=core_send.at[j, sem],
+            recv_sem=core_recv.at[j, sem],
             device_id=other_core,
             device_id_type=MESH,
         )
@@ -472,34 +472,58 @@
             device_id_type=MESH,
         )
 
-    def send_rows(j):
-        cored[j].wait_recv()
-        row_out[j] = (kept[j] + core_in[j].astype(jnp.float32)).astype(jnp.bfloat16)
-        for step in range(1, spans):
-            rowed.append(to_row(j, step))
-            rowed[-1].start()
-
-    for j in range(per):
-        token_finish(1, ff_all, j)
-        normed_ff = ff_all[j].reshape(tokens, width)
+    def transition_in(normed_ff):
         gate = dot(normed_ff, w_in_all[:, 0].reshape(width, units))
         up = dot(normed_ff, w_in_all[:, 1].reshape(width, units))
-        hidden = (gate / (1.0 + jnp.exp(-gate)) * up).astype(jnp.bfloat16)
+        return (gate / (1.0 + jnp.exp(-gate)) * up).astype(jnp.bfloat16)
+
+    def transition_out(j, spans_of, count, sem, hidden):
+        update = dot_t(hidden, w_out_all[...].reshape(width, units))
+        update = update.reshape(count, 2, rows, width)
+        core_out[j, spans_of] = jnp.where(is_low, update[:, 1], update[:, 0]).astype(jnp.bfloat16)
+        cored.append(to_core(j, spans_of, sem))
+        cored[-1].start()
+        return cored[-1], jnp.where(is_low, update[:, 0], update[:, 1])
+
+    def add_core(j, spans_of, copy, kept):
+        copy.wait_recv()
+        row_out[j, spans_of] = (kept + core_in[j, spans_of].astype(jnp.float32)).astype(
+            jnp.bfloat16
+        )
+
+    def send_row(j, step):
+        rowed.append(to_row(j, step))
+        rowed[-1].start()
+
+    def span_transition(j, step):
+        at = span_peer(step)
+        normed_ff = ff_all[j, pl.ds(at * 2, 2)].reshape(2 * rows, width)
+        return transition_out(j, pl.ds(at, 1), 1, step, transition_in(normed_ff))
+
+    whole = pl.ds(0, spans)
+    waiting = []
+    for j in range(per - 1):
+        token_finish(1, ff_all, j)
+        hidden = transition_in(ff_all[j].reshape(tokens, width))
         if j == 0:
             if lines > 2:
                 relay(2, last)
             finish(2)
-        if j + 1 == per - 1:
-            token_forward(1, ff_all, per - 1)
-        if j > 0:
-            send_rows(j - 1)
-        update = dot_t(hidden, w_out_all[...].reshape(width, units))
-        update = update.reshape(spans, 2, rows, width)
-        core_out[j] = jnp.where(is_low, update[:, 1], update[:, 0]).astype(jnp.bfloat16)
-        cored.append(to_core(j))
-        cored[j].start()
-        kept.append(jnp.where(is_low, update[:, 0], update[:, 1]))
-    send_rows(per - 1)
+        waiting.append(transition_out(j, whole, spans, 0, hidden))
+    final = per - 1
+    token_finish(1, ff_all, final, range(1))
+    near = span_transition(final, 0)
+    token_forward(1, ff_all, final)
+    for j in range(final):
+        add_core(j, whole, *waiting[j])
+        for step in range(1, spans):
+            send_row(j, step)
+    token_finish(1, ff_all, final, range(1, spans))
+    far = [span_transition(final, step) for step in range(1, spans)]
+    for step, item in enumerate(far, 1):
+        add_core(final, pl.ds(span_peer(step), 1), *item)
+        send_row(final, step)
+    add_core(final, pl.ds(span, 1), *near)
     for j in range(per):
         stream = streams[j] + row_out[j, span].astype(jnp.float32)
         for step in range(1, spans):
@@ -558,8 +582,8 @@
             dma((2, per, cells)),
             dma((2, per, spans)),
             dma((2, per, spans)),
-            dma((per,)),
-            dma((per,)),
+            dma((per, spans)),
+            dma((per, spans)),
             dma((per, spans)),
             dma((per, spans)),
             dma,

time: 55.8 us -> 55.8 us (level)
  no operation moved by 1% of the time
where the time goes in v3:
time: 55.8 us; the launch traced here: 55.7 us
  Pallas kernels  54 us (97%)
  local copies, waits for them, and re-layouts  1.62 us (3%)
    pallas_call x1, Pallas kernels, fused_body(): pl.pallas_call(block_kernel, out_shape=jax.ShapeDtypeStruct(states.shape,...  54 us
    unnamed x1, local copies, waits for them, and re-layouts  1.62 us

profile of v3, /device:TPU:0, one launch (start us, length us, event | category | flops | bytes accessed | tf_op | source)
XLA Modules:
  0.0 55.7 jit_solution(1860430196714482843)
XLA Ops:
  0.0 54.0 %shard_map.100 = bf16[2,64,768]{2,1,0:T(8,128)(2,1)} custom-call(bf16[2,64,768]{2,1,0:T(8,128)(2,1)} %states_ref.1, s32[2]{0:T(128)} %ancestors_ref.1, bf16[1024,256]{1,0:T(8,128)(2,1)} %bitcast.1, s32[256]{0:T(256)} %mask_ref.1, f32[768]{0:T(1024)} %gain_attn_ref.1, bf16[768,2304]{1,0:T(8,128)(2,1)} %w_qkv_hbm.1, bf16[768,768]{1,0:T(8,128)(2,1)} %w_o_hbm.1, ...), custom_call_target="tpu_custom_call" | custom-call | tf_op jit(solution)/shard_map/pallas_call | solution.py:554
  54.0 1.6 %copy.12 = bf16[2,64,768]{2,1,0:T(8,128)(2,1)} copy(bf16[2,64,768]{2,1,0:T(8,128)(2,1)} %shard_map.100) | data formatting | bytes 393216

commit v4 on v2

--- a/solution.py
+++ b/solution.py
@@ -318,10 +318,12 @@
         @pl.when(jnp.logical_and(line == step, line < last))
         def _():
             remote(1, line, right_sem, above).start()
+            remote(2, line, right_sem, above).start()
 
         @pl.when(jnp.logical_and(line == last - step, line > 0))
         def _():
             remote(1, line, left_sem, below).start()
+            remote(2, line, left_sem, below).start()
 
     wish = to_across(wish_out, wish_in, wish_send, wish_recv)
     wish.start()
@@ -385,9 +387,10 @@
     token_finish(0, normed_all, 0, range(1))
     make_span_keys(0, 0)
     token_forward(0, normed_all, 0)
+    if lines > 1:
+        relay(2, 1)
     for step in range(2, last):
         relay(1, step)
-    relay(2, 0, cross=False)
 
     usable = mask_ref[...].reshape(1, -1) > 0
     half = 8
@@ -430,20 +433,19 @@
         make_span_keys(0, step)
     for j in range(1, per):
         token_forward(0, normed_all, j)
+    for step in range(2, last):
+        relay(2, step)
     locals_[4].wait()
     attended = attend(0)
     locals_[5].wait()
     close(0, attended)
     if lines > 2:
         relay(1, last)
-    if lines > 1:
-        relay(2, 1)
     for j in range(1, per):
         token_finish(0, normed_all, j)
         make_keys(j)
-        if j == 1:
-            for step in range(2, last):
-                relay(2, step)
+        if j == 1 and lines > 2:
+            relay(2, last)
         attended = attend(j)
         token_forward(1, ff_all, j - 1)
         close(j, attended)
@@ -486,8 +488,6 @@
         up = dot(normed_ff, w_in_all[:, 1].reshape(width, units))
         hidden = (gate / (1.0 + jnp.exp(-gate)) * up).astype(jnp.bfloat16)
         if j == 0:
-            if lines > 2:
-                relay(2, last)
             finish(2)
         if j + 1 == per - 1:
             token_forward(1, ff_all, per - 1)

time: 55.8 us -> 55.5 us (level)
  no operation moved by 1% of the time
where the time goes in v4:
time: 55.5 us; the launch traced here: 55.4 us
  Pallas kernels  53.8 us (97%)
  local copies, waits for them, and re-layouts  1.62 us (3%)
    pallas_call x1, Pallas kernels, fused_body(): pl.pallas_call(block_kernel, out_shape=jax.ShapeDtypeStruct(states.shape,...  53.8 us
    unnamed x1, local copies, waits for them, and re-layouts  1.62 us

profile of v4, /device:TPU:0, one launch (start us, length us, event | category | flops | bytes accessed | tf_op | source)
XLA Modules:
  0.0 55.4 jit_solution(689200034186877147)
XLA Ops:
  0.0 53.8 %shard_map.100 = bf16[2,64,768]{2,1,0:T(8,128)(2,1)} custom-call(bf16[2,64,768]{2,1,0:T(8,128)(2,1)} %states_ref.1, s32[2]{0:T(128)} %ancestors_ref.1, bf16[1024,256]{1,0:T(8,128)(2,1)} %bitcast.1, s32[256]{0:T(256)} %mask_ref.1, f32[768]{0:T(1024)} %gain_attn_ref.1, bf16[768,2304]{1,0:T(8,128)(2,1)} %w_qkv_hbm.1, bf16[768,768]{1,0:T(8,128)(2,1)} %w_o_hbm.1, ...), custom_call_target="tpu_custom_call" | custom-call | tf_op jit(solution)/shard_map/pallas_call | solution.py:530
  53.8 1.6 %copy.12 = bf16[2,64,768]{2,1,0:T(8,128)(2,1)} copy(bf16[2,64,768]{2,1,0:T(8,128)(2,1)} %shard_map.100) | data formatting | bytes 393216

commit v5 on v4

--- a/solution.py
+++ b/solution.py
@@ -175,10 +175,11 @@
     )
 
     views = (
-        lambda k: states_all.at[pl.ds(k * per, per)],
+        lambda k: states_all.at[k * per],
         lambda k: w_in_all.at[k],
         lambda k: w_out_all.at[k],
-    )
+    ) + tuple(lambda k, i=i: states_all.at[k * per + i] for i in range(1, per))
+    state_kinds = (0,) + tuple(range(3, 2 + per))
 
     def remote(kind, source, sems, device):
         k = source * 2 + side
@@ -222,7 +223,7 @@
             def _():
                 remote(kind, high, left_sem, below).start()
 
-        if kind == 0 or not cross:
+        if kind in state_kinds or not cross:
             return
 
         @pl.when(low >= 0)
@@ -241,7 +242,7 @@
 
     def drain(kind):
         for source in range(lines):
-            if kind > 0:
+            if kind not in state_kinds:
                 remote(kind, source, across_sem, across).wait_send()
 
             @pl.when(jnp.logical_and(line < lines - 1, source <= line))
@@ -327,7 +328,8 @@
 
     wish = to_across(wish_out, wish_in, wish_send, wish_recv)
     wish.start()
-    relay(0, 0)
+    for kind in state_kinds:
+        relay(kind, 0)
     locals_[1].wait()
     relay(1, 0, along=False)
     locals_[2].wait()
@@ -344,7 +346,8 @@
     nothing = jnp.zeros((rows, width), jnp.float32)
     asked = [pick_from(nothing, wish_in[j], line) for j in range(per)]
     for step in range(1, lines):
-        relay(0, step)
+        for kind in state_kinds:
+            relay(kind, step)
         own_weights_along(step)
         for source in (jnp.maximum(line - step, 0), jnp.minimum(line + step, last)):
             if step < last:
@@ -508,7 +511,7 @@
         out_ref[j] = stream.astype(jnp.bfloat16)
     for copy in sent + cored + rowed + [wish] + picks:
         copy.wait_send()
-    for kind in range(3):
+    for kind in range(2 + per):
         drain(kind)
 
 
@@ -551,10 +554,10 @@
             pltpu.VMEM((per, rows, width), bf16),
             pltpu.VMEM((per, rows, width), bf16),
             dma((6,)),
-            dma((3, groups)),
-            dma((3, lines)),
-            dma((3, lines)),
-            dma((3, lines)),
+            dma((2 + per, groups)),
+            dma((2 + per, lines)),
+            dma((2 + per, lines)),
+            dma((2 + per, lines)),
             dma((2, per, cells)),
             dma((2, per, spans)),
             dma((2, per, spans)),

time: 55.5 us -> 53.2 us (0.959)
  Pallas kernels: 53.8 us -> 51.5 us
    pallas_call x1, Pallas kernels: 53.8 us -> 51.5 us  [fused_body(): pl.pallas_call(block_kernel, out_shape=jax.ShapeDtypeStruct(states.shape,...]
where the time goes in v5:
time: 53.2 us; the launch traced here: 53.1 us
  Pallas kernels  51.5 us (97%)
  local copies, waits for them, and re-layouts  1.62 us (3%)
    pallas_call x1, Pallas kernels, fused_body(): pl.pallas_call(block_kernel, out_shape=jax.ShapeDtypeStruct(states.shape,...  51.5 us
    unnamed x1, local copies, waits for them, and re-layouts  1.62 us

profile of v5, /device:TPU:0, one launch (start us, length us, event | category | flops | bytes accessed | tf_op | source)
XLA Modules:
  0.0 53.1 jit_solution(13792551925272360736)
XLA Ops:
  0.0 51.5 %shard_map.100 = bf16[2,64,768]{2,1,0:T(8,128)(2,1)} custom-call(bf16[2,64,768]{2,1,0:T(8,128)(2,1)} %states_ref.1, s32[2]{0:T(128)} %ancestors_ref.1, bf16[1024,256]{1,0:T(8,128)(2,1)} %bitcast.1, s32[256]{0:T(256)} %mask_ref.1, f32[768]{0:T(1024)} %gain_attn_ref.1, bf16[768,2304]{1,0:T(8,128)(2,1)} %w_qkv_hbm.1, bf16[768,768]{1,0:T(8,128)(2,1)} %w_o_hbm.1, ...), custom_call_target="tpu_custom_call" | custom-call | tf_op jit(solution)/shard_map/pallas_call | solution.py:533
  51.5 1.6 %copy.12 = bf16[2,64,768]{2,1,0:T(8,128)(2,1)} copy(bf16[2,64,768]{2,1,0:T(8,128)(2,1)} %shard_map.100) | data formatting | bytes 393216
